TPU v7x, 32 devices: a whole 2x2x4 slice. The times are simulated.
32 devices in a mesh: prow: 4 (over x, core), pcol: 8 (over z, y).
Axes of the slice: x: 2, y: 2, z: 4, core: 2. Of those that a mesh axis runs over, the one named last changes fastest.
Arguments:
- tail_factor: float32 [63488, 2048], P(('prow', 'pcol')), may hold values from -0.0234375 to 0.0234375
- link_factor: float32 [1024, 1024], P(('prow', 'pcol')), may hold values from -0.1875 to 0.1875
- diag_inverse: float32 [2, 1024, 1024], P(None, ('prow', 'pcol')), as said below
- tail_solution: float32 [63488, 256], P(('prow', 'pcol')), may hold values from -6 to 6
- head_rhs: float32 [2, 1024, 256], P(None, ('prow', 'pcol')), may hold values from -6 to 6
- head_pivots: int32 [2, 1024], P(None, ('prow', 'pcol')), may hold values from 0 to 65535, as said below
- tail_pivots: int32 [63488], P(('prow', 'pcol')), may hold values from 0 to 65535, as said below
Outputs:
- solution: float32 [65536, 256], P(('prow', 'pcol'))
Inputs may be any that keep to these rules, and one draw needn't show every extreme that they name: head_pivots and tail_pivots together are a permutation of the 65536 rows. Split the rows into 32 sets, set s holding rows s * 32 to (s + 1) * 32 - 1 of each head block and rows s * 1984 to (s + 1) * 1984 - 1 of tail_pivots, and the final rows into aligned blocks of 2048: each set sends at most 85 rows into each block, and every set sends exactly 85 into some block. `head_pivots`: part of the same permutation as tail_pivots. `diag_inverse`: unit upper triangular.
All inputs are finite; a program needn't handle non-finite values.
Results may differ from a plain program's by a relative error of at most 0.00007.
Values sent between devices are 32-bit elements; how exact they have to be, the bound alone decides.
A program may use at most 128 MiB of HBM per device.

v0:
```python
import jax
import jax.numpy as jnp
from jax import lax
from jax.sharding import PartitionSpec as P


def body(tail_factor, link_factor, diag_inverse, tail_solution, head_rhs, head_pivots, tail_pivots):
    highest = lax.Precision.HIGHEST
    block_rows = diag_inverse.shape[2]
    head_rows = diag_inverse.shape[1]
    columns = tail_solution.shape[1]
    devices = lax.axis_size(("prow", "pcol"))
    position = lax.axis_index(("prow", "pcol"))
    offset = position * head_rows
    blank = jnp.zeros((block_rows, columns), jnp.float32)
    tail_terms = jnp.einsum("jc,jr->cr", tail_factor, tail_solution, precision=highest)
    own_upper = lax.dynamic_update_slice(blank, head_rhs[1], (offset, 0))
    own_lower = lax.dynamic_update_slice(blank, head_rhs[0], (offset, 0))
    upper_term = own_upper - tail_terms[block_rows:]
    lower_base = own_lower - tail_terms[:block_rows]
    reduced_upper = lax.psum(upper_term, ("prow", "pcol"))
    upper = jnp.dot(diag_inverse[1], reduced_upper, precision=highest)
    lower_term = lower_base - jnp.einsum("ic,ir->cr", link_factor, upper, precision=highest)
    reduced_lower = lax.psum(lower_term, ("prow", "pcol"))
    lower = jnp.dot(diag_inverse[0], reduced_lower, precision=highest)
    solved_rows = jnp.concatenate([lower, upper, tail_solution], axis=0)
    destinations = jnp.concatenate([head_pivots[0], head_pivots[1], tail_pivots])
    rows_each = solved_rows.shape[0]
    even_count = rows_each // devices
    capacity = even_count + max(even_count // 3, 1)
    owner_dev = destinations // rows_each
    local_row = destinations % rows_each
    one_hot = (owner_dev[:, None] == jnp.arange(devices, dtype=jnp.int32)[None, :]).astype(
        jnp.int32
    )
    earlier = jnp.cumsum(one_hot, axis=0) - one_hot
    rank_in_pair = jnp.sum(earlier * one_hot, axis=1)
    outgoing = (
        jnp.zeros((devices, capacity, columns), jnp.float32)
        .at[owner_dev, rank_in_pair]
        .set(solved_rows)
    )
    slot_index = (
        jnp.full((devices, capacity), rows_each, jnp.int32)
        .at[owner_dev, rank_in_pair]
        .set(local_row)
    )
    received, landing = (
        lax.all_to_all(outgoing, ("prow", "pcol"), split_axis=0, concat_axis=0, tiled=True),
        lax.all_to_all(slot_index, ("prow", "pcol"), split_axis=0, concat_axis=0, tiled=True),
    )
    flat_rows = received.reshape(-1, columns)
    flat_slots = landing.reshape(-1)
    return jnp.zeros((rows_each, columns), jnp.float32).at[flat_slots].set(flat_rows, mode="drop")


def solution(mesh):
    return jax.shard_map(
        body,
        mesh=mesh,
        in_specs=(
            P(("prow", "pcol"), None),
            P(("prow", "pcol"), None),
            P(None, ("prow", "pcol"), None),
            P(("prow", "pcol"), None),
            P(None, ("prow", "pcol"), None),
            P(None, ("prow", "pcol")),
            P(("prow", "pcol")),
        ),
        out_specs=P(("prow", "pcol"), None),
        check_vma=False,
    )
```

profile of v0, /device:TPU:0, one launch (start us, length us, event | category | flops | bytes accessed | tf_op | source)
XLA Modules:
  0.0 416.9 jit_solution(7344742650952042798)
XLA Ops:
  6.5 29.2 %fusion.26 = f32[2048,256]{1,0:T(8,128)S(1)} fusion(f32[1984,2048]{1,0:T(8,128)} %param.7, f32[1984,256]{1,0:T(8,128)} %param.10), kind=kOutput, calls=%fused_computation.67 | convolution fusion | flops 12482248704 | bytes 20381696 | tf_op jit(solution)/shard_map/jc,jr->cr/dot_general | solution.py:16
  35.9 1.1 slice_subtract_fusion
  37.1 0.1 concatenate.61
  37.3 9.1 %reduce-window.6 = s32[32,16,128]{2,1,0:T(8,128)S(1)} reduce-window(s32[32,16,128]{2,1,0:T(8,128)S(1)} %fusion.13, s32[]{:T(128)} %constant.48.clone.1), window={size=1x1x128 pad=0_0x0_0x127_0}, to_apply=%region_0.0 | reduce-window | flops 8323072 | bytes 524292 | tf_op jit(solution)/shard_map/reduce-window
  46.3 0.1 slice.40
  46.5 0.2 copy.16
  46.7 0.2 reduce-window.9
  46.9 0.1 broadcast_add_fusion
  47.4 122.4 %all-reduce.3.cloned.1.call-done = f32[1024,256]{1,0:T(8,128)} async-done(((f32[1024,256]{1,0:T(8,128)}), f32[1024,256]{1,0:T(8,128)}) %all-reduce.3.cloned.1.call-update) | async-done | bytes 1048592 | tf_op jit(solution)/shard_map/psum | solution.py:21
  169.8 1.9 fusion.15
  171.7 2.0 fusion.7
  174.1 8.1 %scatter_custom_fusion.1 = s32[2720]{0:T(1024)S(1)} fusion(s32[2048]{0:T(1024)S(1)} %get-tuple-element.10, s32[2048]{0:T(1024)S(1)} %get-tuple-element.7, s32[]{:T(128)} %constant.46.clone.1), kind=kCustom, calls=%fused_computation.58 | custom fusion | bytes 10884
  182.2 0.7 all_to_all.9
  182.9 3.7 all-to-all-start
  186.6 118.1 %all-reduce.5.cloned.1.call-done = f32[1024,256]{1,0:T(8,128)} async-done(((f32[1024,256]{1,0:T(8,128)}), f32[1024,256]{1,0:T(8,128)}) %all-reduce.5.cloned.1.call-update) | async-done | bytes 1048592 | tf_op jit(solution)/shard_map/psum | solution.py:24
  304.7 1.9 convolution_bitcast_fusion.1
  306.6 10.3 %scatter_custom_fusion.2 = f32[2720,256]{1,0:T(8,128)S(1)} fusion(s32[2048]{0:T(1024)S(1)} %get-tuple-element.9, f32[1984,256]{1,0:T(8,128)} %param.10, f32[]{:T(128)} %constant.76, f32[32,256]{1,0:T(8,128)S(1)} %bitcast.59, f32[32,256]{1,0:T(8,128)S(1)} %convolution_bitcast_fusion.1, f32[]{:T(128)} %constant.27.clone.1), kind=kCustom, calls=%fused_computation.3 | custom fusion | flops 1048576 | bytes 4882440
  316.9 3.2 copy.14
  320.1 3.6 all-to-all-start.1
  323.7 0.5 broadcast.191
  324.2 0.7 reduce.12
  325.0 66.0 %all-to-all-done.1 = f32[32,85,256]{2,1,0:T(8,128)S(1)} async-done(((f32[32,85,256]{2,1,0:T(8,128)}), f32[32,85,256]{2,1,0:T(8,128)S(1)}, u32[]{:S(2)}, u32[]{:S(2)}) %all-to-all-start.1) | async-done | bytes 2785312 | tf_op jit(solution)/shard_map/all_to_all | solution.py:49
  391.1 1.7 reshape.338
  392.8 17.2 %scatter_custom_fusion = f32[2048,256]{1,0:T(8,128)} fusion(s32[2720]{0:T(1024)S(1)} %fusion.19, f32[2720,256]{1,0:T(8,128)} %reshape.338, f32[]{:T(128)} %constant.27.clone.1), kind=kCustom, calls=%fused_computation.15 | custom fusion | bytes 2097664 | tf_op jit(solution)/shard_map/scatter | solution.py:54
  (35 shorter events, 0.9 us)
Async XLA Ops:
  6.5 165.2 %copy-start = (f32[32,1024]{1,0:T(8,128)S(1)}, f32[32,1024]{1,0:T(8,128)}, u32[]{:S(2)}) copy-start(f32[32,1024]{1,0:T(8,128)} %param.8) | copy-start | bytes 393220
  6.5 163.3 %all-reduce.3.cloned.1.call-start = ((), (), s32[]{:S(2)}) async-start(), calls=%async_computation.2 | async-start | bytes 2097152 | tf_op jit(solution)/shard_map/psum | solution.py:21
  6.5 29.3 %copy-start.1 = (f32[2,32,256]{2,1,0:T(8,128)S(1)}, f32[2,32,256]{2,1,0:T(8,128)}, u32[]{:S(2)}) copy-start(f32[2,32,256]{2,1,0:T(8,128)} %param.11) | copy-start | bytes 196612
  35.9 1.2 copy-start.3
  35.9 1.2 copy-start.2
  37.0 267.7 %all-reduce.5.cloned.1.call-start = ((), (), s32[]{:S(2)}) async-start(), calls=%async_computation.3 | async-start | bytes 2097152 | tf_op jit(solution)/shard_map/psum | solution.py:24
  171.7 2.1 copy-start.6
  171.7 2.2 copy-start.4
  171.7 2.2 copy-start.5
  182.9 137.2 %all-to-all-start = ((s32[32,1,85]{2,1,0:T(1,128)}), s32[32,1,85]{2,1,0:T(1,128)S(1)}, u32[]{:S(2)}, u32[]{:S(2)}) async-start(s32[32,1,85]{2,1,0:T(1,128)} %all_to_all.9), calls=%async_computation | async-start | bytes 32768 | tf_op jit(solution)/shard_map/all_to_all | solution.py:50
  320.1 71.0 %all-to-all-start.1 = ((f32[32,85,256]{2,1,0:T(8,128)}), f32[32,85,256]{2,1,0:T(8,128)S(1)}, u32[]{:S(2)}, u32[]{:S(2)}) async-start(f32[32,85,256]{2,1,0:T(8,128)} %copy.14), calls=%async_computation.1 | async-start | bytes 5767168 | tf_op jit(solution)/shard_map/all_to_all | solution.py:49
Sparse Core Ops, SparseCore 0:
  37.1 132.6 all-reduce.2
  175.8 128.8 all-reduce.4
where the time goes:
time: 417 us
  waiting for transfers between devices  307 us (74%)
  matrix products  35 us (8%)
  local copies, waits for them, and re-layouts  32.3 us (8%)
  other arithmetic  22 us (5%)
  between operations  13.7 us (3%)
  starting transfers between devices  7.35 us (2%)
    psum x1, waiting for transfers between devices, body(): reduced_upper = lax.psum(upper_term, ('prow', 'pcol'))  122 us
    psum x1, waiting for transfers between devices, body(): reduced_lower = lax.psum(lower_term, ('prow', 'pcol'))  118 us
    all_to_all x1, waiting for transfers between devices, body(): lax.all_to_all(outgoing, ('prow', 'pcol'), split_axis=0, concat_axis=0, t...  66 us
    dot_general x1, matrix products, body(): jnp.einsum('jc,jr->cr', tail_factor, tail_solution, precision=highest)  29.2 us
    scatter x1, local copies, waits for them, and re-layouts, body(): jnp.zeros((rows_each, columns), jnp.float32).at[flat_slots]  17.2 us
    unnamed x4, other arithmetic  10.5 us
    another operation x3, other arithmetic  9.41 us
  transfers between devices with their start and end apart: 4, of which 3 were waited for; matrix products, arithmetic and copies ran while one was open for 8% of the time, Pallas kernels for 0%

commit v1 on v0

v1 whole, which is shorter than its diff:
```python
import functools

import jax
import jax.numpy as jnp
from jax import lax
from jax.experimental import pallas as pl
from jax.experimental.pallas import tpu as pltpu
from jax.sharding import PartitionSpec as P

AXES = ("prow", "pcol")
MESH = pl.DeviceIdType.MESH
HIGHEST = lax.Precision.HIGHEST


def levels_of(prow, pcol):
    cores = 2 if prow % 2 == 0 else 1
    depth = 4 if pcol % 4 == 0 else 1
    return prow // cores, cores, depth, pcol // depth


def dot32(a, b, contract):
    return lax.dot_general(
        a, b, (contract, ((), ())), precision=HIGHEST, preferred_element_type=jnp.float32
    )


def sweep_kernel(
    sizes, terms, link, diag, rhs, pivots, outgoing,
    received, heads, all_pivots,
    full_upper, full_lower, base, pick,
    up_recv, up_sum, low_recv, low_sum,
    send_sems, recv_sems, move_send, move_recv, own_sem,
):
    xs, cores, zs, ys = sizes
    prow, pcol = lax.axis_index("prow"), lax.axis_index("pcol")
    devices = xs * cores * zs * ys
    position = prow * (zs * ys) + pcol
    x, core = prow // cores, prow % cores
    z, y = pcol // ys, pcol % ys

    def at_core(v):
        return (x * cores + v, pcol)

    def at_x(v):
        return (v * cores + core, pcol)

    def at_y(v):
        return (prow, z * ys + v)

    def at_z(v):
        return (prow, v * ys + y)

    coords = {"c": (core, cores, at_core), "x": (x, xs, at_x), "y": (y, ys, at_y), "z": (z, zs, at_z)}
    counter = [0]

    def remote(src, dst, device):
        k = counter[0]
        counter[0] += 1
        copy = pltpu.make_async_remote_copy(
            src_ref=src, dst_ref=dst, send_sem=send_sems.at[k], recv_sem=recv_sems.at[k],
            device_id=device, device_id_type=MESH,
        )
        copy.start()
        return copy

    def reduce_start(axis, source, cut, landing):
        me, size, place = coords[axis]
        return [
            remote(cut(source, (me + d) % size), landing.at[d - 1], place((me + d) % size))
            for d in range(1, size)
        ]

    def gather_start(axis, ref):
        size = coords[axis][1]
        me, _, place = coords[axis]
        part = {
            "z": ref.at[x, core, z, y],
            "y": ref.at[x, core, :, y],
            "x": ref.at[x, core],
            "c": ref.at[:, core],
        }[axis]
        return [remote(part, part, place((me + d) % size)) for d in range(1, size)]

    def finish(copies):
        for copy in copies:
            copy.wait()

    cuts = {
        "c": lambda ref, v: ref.at[:, v],
        "x": lambda ref, v: ref.at[v],
        "y": lambda ref, v: ref.at[:, v],
        "z": lambda ref, v: ref.at[v],
    }
    reads = {
        "c": lambda ref: ref[:, core],
        "x": lambda ref: ref[x],
        "y": lambda ref: ref[:, y],
        "z": lambda ref: ref[z],
    }

    def reduce_levels(source, landings, sums, beside):
        current = source
        for step, axis in enumerate("cxyz"):
            size = coords[axis][1]
            copies = reduce_start(axis, current, cuts[axis], landings[step])
            others = [gather_start("zyxc"[step], ref) for ref in beside]
            finish(copies)
            total = reads[axis](current)
            for d in range(1, size):
                total = total + landings[step][d - 1]
            sums[step][...] = total
            for more in others:
                finish(more)
            current = sums[step]
        return current

    barrier = pltpu.get_barrier_semaphore()

    def greet(d, carry):
        peer = (position + d) % devices
        pl.semaphore_signal(
            barrier, inc=1, device_id=(peer // (zs * ys), peer % (zs * ys)), device_id_type=MESH
        )
        return carry

    lax.fori_loop(1, devices, greet, 0)
    pl.semaphore_wait(barrier, devices - 1)

    def move(d):
        peer = (position + d) % devices
        return pltpu.make_async_remote_copy(
            src_ref=outgoing.at[peer], dst_ref=received.at[position],
            send_sem=move_send.at[d], recv_sem=move_recv.at[d],
            device_id=(peer // (zs * ys), peer % (zs * ys)), device_id_type=MESH,
        )

    def move_start(d, carry):
        move(d).start()
        return carry

    def move_wait(d, carry):
        move(d).wait()
        return carry

    own = pltpu.make_async_copy(outgoing.at[position], received.at[position], own_sem)
    own.start()
    lax.fori_loop(1, devices, move_start, 0)

    all_pivots[x, core, z, y] = pivots[...]
    reduced = reduce_levels(terms.at[1], up_recv, up_sum, [all_pivots])
    full_upper[x, core, z, y] = rhs[1] - reduced[...]
    for axis in "zyxc":
        finish(gather_start(axis, full_upper))
    rows = devices * rhs.shape[1]
    columns = rhs.shape[2]
    upper = dot32(diag[1], full_upper[...].reshape(rows, columns), ((1,), (0,)))
    heads[1, x, core, z, y] = upper
    base[...] = terms[0] + dot32(link[...], upper, ((0,), (0,))).reshape(base.shape)
    reduced = reduce_levels(base, low_recv, low_sum, [heads.at[1]])
    full_lower[x, core, z, y] = rhs[0] - reduced[...]
    for axis in "zyxc":
        finish(gather_start(axis, full_lower))
    heads[0, x, core, z, y] = dot32(diag[0], full_lower[...].reshape(rows, columns), ((1,), (0,)))
    for axis in "zyxc":
        finish(gather_start(axis, heads.at[0]))

    own.wait()
    lax.fori_loop(1, devices, move_wait, 0)


def sweep_call(sizes, terms, link, diag, rhs, pivots, outgoing):
    xs, cores, zs, ys = sizes
    devices = xs * cores * zs * ys
    _, share, columns = rhs.shape
    tail = (share, columns)
    landings = lambda: [
        pltpu.VMEM((max(cores - 1, 1), xs, zs, ys) + tail, jnp.float32),
        pltpu.VMEM((max(xs - 1, 1), zs, ys) + tail, jnp.float32),
        pltpu.VMEM((max(ys - 1, 1), zs) + tail, jnp.float32),
        pltpu.VMEM((max(zs - 1, 1),) + tail, jnp.float32),
    ]
    sums = lambda: [
        pltpu.VMEM((xs, zs, ys) + tail, jnp.float32),
        pltpu.VMEM((zs, ys) + tail, jnp.float32),
        pltpu.VMEM((zs,) + tail, jnp.float32),
        pltpu.VMEM(tail, jnp.float32),
    ]
    whole = (xs, cores, zs, ys) + tail
    copies = 7 * ((cores - 1) + (xs - 1) + (zs - 1) + (ys - 1))
    vmem = pl.BlockSpec(memory_space=pltpu.VMEM)
    anywhere = pl.BlockSpec(memory_space=pl.ANY)
    return pl.pallas_call(
        functools.partial(sweep_kernel, sizes),
        out_shape=(
            jax.ShapeDtypeStruct(outgoing.shape, jnp.float32),
            jax.ShapeDtypeStruct((2,) + whole, jnp.float32),
            jax.ShapeDtypeStruct((xs, cores, zs, ys) + pivots.shape, jnp.int32),
        ),
        in_specs=[vmem] * 5 + [anywhere],
        out_specs=(anywhere, vmem, vmem),
        scratch_shapes=[
            pltpu.VMEM(whole, jnp.float32),
            pltpu.VMEM(whole, jnp.float32),
            pltpu.VMEM(whole, jnp.float32),
            pltpu.VMEM(tail, jnp.float32),
            landings(), sums(), landings(), sums(),
            pltpu.SemaphoreType.DMA((copies,)),
            pltpu.SemaphoreType.DMA((copies,)),
            pltpu.SemaphoreType.DMA((devices,)),
            pltpu.SemaphoreType.DMA((devices,)),
            pltpu.SemaphoreType.DMA,
        ],
        compiler_params=pltpu.CompilerParams(
            collective_id=0, has_side_effects=True, vmem_limit_bytes=40 * 2**20
        ),
    )(terms, link, diag, rhs, pivots, outgoing)


def pack_kernel(capacity, slots, rows, index_rows, out):
    def step(group, carry):
        start = pl.multiple_of(group * 8, 8)
        for k in range(8):
            out[pl.ds(slots[start + k], 1), :] = rows[pl.ds(start + k, 1), :]
        return carry

    lax.fori_loop(0, rows.shape[0] // 8, step, 0)
    devices = index_rows.shape[0]
    each = out.shape[0] // devices
    for d in range(devices):
        out[pl.ds(d * each + capacity, 1), :] = index_rows[pl.ds(d, 1), :]


def pack_call(capacity, each, slots, rows, index_rows):
    devices, columns = index_rows.shape
    return pl.pallas_call(
        functools.partial(pack_kernel, capacity),
        out_shape=jax.ShapeDtypeStruct((devices * each, columns), jnp.float32),
        in_specs=[
            pl.BlockSpec(memory_space=pltpu.SMEM),
            pl.BlockSpec(memory_space=pltpu.VMEM),
            pl.BlockSpec(memory_space=pltpu.VMEM),
        ],
        out_specs=pl.BlockSpec(memory_space=pltpu.VMEM),
        compiler_params=pltpu.CompilerParams(vmem_limit_bytes=24 * 2**20),
    )(slots, rows, index_rows)


def unpack_kernel(tail_slots, head_slots, received, heads, out, held, sem):
    def place(slots, source):
        def step(group, carry):
            start = pl.multiple_of(group * 8, 8)
            for k in range(8):
                held[pl.ds(slots[start + k], 1), :] = source[pl.ds(start + k, 1), :]
            return carry

        lax.fori_loop(0, source.shape[0] // 8, step, 0)

    place(tail_slots, received)
    place(head_slots, heads)
    copy = pltpu.make_async_copy(held.at[pl.ds(0, out.shape[0])], out, sem)
    copy.start()
    copy.wait()


def unpack_call(rows_each, tail_slots, head_slots, received, heads):
    columns = heads.shape[1]
    smem = pl.BlockSpec(memory_space=pltpu.SMEM)
    vmem = pl.BlockSpec(memory_space=pltpu.VMEM)
    return pl.pallas_call(
        unpack_kernel,
        out_shape=jax.ShapeDtypeStruct((rows_each, columns), jnp.float32),
        in_specs=[smem, smem, vmem, vmem],
        out_specs=pl.BlockSpec(memory_space=pl.ANY),
        scratch_shapes=[pltpu.VMEM((rows_each + 8, columns), jnp.float32), pltpu.SemaphoreType.DMA],
        compiler_params=pltpu.CompilerParams(vmem_limit_bytes=24 * 2**20),
    )(tail_slots, head_slots, received, heads)


def ranks_of(one_hot):
    rows, devices = one_hot.shape
    block = 128
    padded = -(-rows // block) * block
    blocks = jnp.pad(one_hot, ((0, padded - rows), (0, 0))).reshape(-1, block, devices)
    before = jnp.tril(jnp.ones((block, block), jnp.bfloat16), -1)
    inside = jnp.einsum("ij,bjd->bid", before, blocks, preferred_element_type=jnp.float32)
    totals = jnp.sum(blocks.astype(jnp.float32), axis=1)
    ahead = jnp.cumsum(totals, axis=0) - totals
    ranks = (inside + ahead[:, None, :]) * blocks.astype(jnp.float32)
    return jnp.sum(ranks, axis=2).reshape(-1)[:rows].astype(jnp.int32)


def body(tail_factor, link_factor, diag_inverse, tail_solution, head_rhs, head_pivots, tail_pivots):
    block_rows = diag_inverse.shape[2]
    share = diag_inverse.shape[1]
    tail_rows, columns = tail_solution.shape
    sizes = levels_of(lax.axis_size("prow"), lax.axis_size("pcol"))
    devices = lax.axis_size(AXES)
    position = lax.axis_index(AXES)
    rows_each = tail_rows + 2 * share
    even_count = rows_each // devices
    capacity = even_count + max(even_count // 3, 1)
    each = -(-(capacity + 1) // 8) * 8

    owner = tail_pivots // rows_each
    local_row = tail_pivots % rows_each
    one_hot = (owner[:, None] == jnp.arange(devices, dtype=jnp.int32)[None, :]).astype(jnp.bfloat16)
    rank = ranks_of(one_hot)
    slots = owner * each + rank
    at_rank = rank[:, None] == jnp.arange(columns, dtype=jnp.int32)[None, :]
    marked = local_row + 1
    high, low = marked // 64, marked % 64
    put = lambda v: jnp.dot(
        one_hot.T, jnp.where(at_rank, v[:, None], 0).astype(jnp.bfloat16),
        preferred_element_type=jnp.float32,
    )
    index_rows = put(high) * 64.0 + put(low)
    outgoing = pack_call(capacity, each, slots, tail_solution, index_rows)

    terms = jnp.einsum(
        "jc,jr->cr", tail_factor, tail_solution, precision=lax.Precision.HIGH
    )
    own_pivots = jnp.pad(head_pivots, ((0, 6), (0, 128 - share)))
    received, heads, all_pivots = sweep_call(
        sizes,
        terms.reshape((2,) + sizes + (share, columns)),
        link_factor, diag_inverse, head_rhs, own_pivots,
        outgoing.reshape(devices, each, columns),
    )
    marks = received[:, capacity, :each].astype(jnp.int32)
    inner = jnp.arange(each, dtype=jnp.int32)[None, :] < capacity
    tail_slots = jnp.where(inner & (marks > 0), marks - 1, rows_each).reshape(-1)
    pivots = all_pivots.reshape(devices, 8, 128)[:, :2, :share]
    head_slots = jnp.transpose(pivots, (1, 0, 2)).reshape(-1) - position * rows_each
    head_slots = jnp.where((head_slots >= 0) & (head_slots < rows_each), head_slots, rows_each)
    return unpack_call(
        rows_each, tail_slots, head_slots,
        received.reshape(-1, columns), heads.reshape(-1, columns),
    )


def solution(mesh):
    return jax.shard_map(
        body,
        mesh=mesh,
        in_specs=(
            P(AXES, None),
            P(AXES, None),
            P(None, AXES, None),
            P(AXES, None),
            P(None, AXES, None),
            P(None, AXES),
            P(AXES),
        ),
        out_specs=P(AXES, None),
        check_vma=False,
    )
```

time: 417 us -> 214 us (0.51)
  waiting for transfers between devices: 307 us -> 0 us
  Pallas kernels: 0 us -> 190 us
  local copies, waits for them, and re-layouts: 32.3 us -> 3.3 us
  other arithmetic: 22 us -> 1.95 us
  matrix products: 35 us -> 18.5 us
  between operations: 13.7 us -> 0.23 us
  starting transfers between devices: 7.35 us -> 0 us
    psum x2 -> x0, waiting for transfers between devices: 241 us -> none  [the longest x1 122 us: body(): reduced_upper = lax.psum(upper_term, ('prow', 'pcol'))]
    pallas_call x0 -> x3, Pallas kernels: none -> 190 us  [the longest x1 162 us: sweep_call(): pl.pallas_call(functools.partial(sweep_kernel, sizes), out_shape=(jax.Sha...]
    all_to_all x2 -> x0, waiting for transfers between devices: 66 us -> none  [the longest x1 66 us: body(): lax.all_to_all(outgoing, ('prow', 'pcol'), split_axis=0, concat_axis=0, t...]
    scatter x2 -> x0, local copies, waits for them, and re-layouts: 20.4 us -> none  [the longest x1 17.2 us: body(): jnp.zeros((rows_each, columns), jnp.float32).at[flat_slots]]
    dot_general x4, matrix products: 35 us -> 18.5 us  [the longest x1 16.8 us: body(): jnp.einsum('jc,jr->cr', tail_factor, tail_solution, precision=lax.Precisi...]
    unnamed x4 -> x0, other arithmetic: 10.5 us -> none
    another operation x3 -> x1, other arithmetic: 9.41 us -> 0.03 us  [ranks_of(): ahead = jnp.cumsum(totals, axis=0) - totals]
    all_to_all x2 -> x0, starting transfers between devices: 7.31 us -> none  [the longest x1 3.75 us: body(): lax.all_to_all(slot_index, ('prow', 'pcol'), split_axis=0, concat_axis=0,...]
  transfers between devices with their start and end apart: 4 -> 0, of which waited for: 3 -> 0; matrix products, arithmetic and copies ran while one was open for 8% -> 0% of each run, Pallas kernels for 0% -> 0%
where the time goes in v1:
time: 214 us
  Pallas kernels  190 us (89%)
  matrix products  18.5 us (9%)
  local copies, waits for them, and re-layouts  3.3 us (2%)
    pallas_call x1, Pallas kernels, sweep_call(): pl.pallas_call(functools.partial(sweep_kernel, sizes), out_shape=(jax.Sha...  162 us
    pallas_call x1, Pallas kernels, unpack_call(): pl.pallas_call(unpack_kernel, out_shape=jax.ShapeDtypeStruct((rows_each,...  19.8 us
    dot_general x1, matrix products, body(): jnp.einsum('jc,jr->cr', tail_factor, tail_solution, precision=lax.Precisi...  16.8 us
    pallas_call x1, Pallas kernels, pack_call(): pl.pallas_call(functools.partial(pack_kernel, capacity), out_shape=jax.Sh...  7.73 us

profile of v1, /device:TPU:0, one launch (start us, length us, event | category | flops | bytes accessed | tf_op | source)
XLA Modules:
  0.0 213.8 jit_solution(950774534833343242)
XLA Ops:
  0.0 0.7 add_select_fusion.3
  0.8 0.0 copy-start
  0.8 0.1 convert_reduce_fusion
  1.0 0.3 fusion.2
  1.2 0.8 add_select_fusion
  2.1 0.7 convolution_multiply_fusion
  2.8 0.7 convolution_add_fusion.1.index_rows
  3.5 7.7 %shard_map.73 = f32[2816,256]{1,0:T(8,128)S(1)} custom-call(s32[1984]{0:T(1024)S(1)} %get-tuple-element.12.slots, f32[1984,256]{1,0:T(8,128)S(1)} %copy-done, f32[32,256]{1,0:T(8,128)S(1)} %convolution_add_fusion.1.index_rows), custom_call_target="tpu_custom_call" | custom-call | tf_op jit(solution)/shard_map/pallas_call | solution.py:235
  11.3 0.0 copy-start.6
  11.3 0.0 copy-start.3
  11.3 0.0 copy-start.4
  11.3 0.0 copy-start.5
  11.3 16.8 %fusion.29 = f32[2048,256]{1,0:T(8,128)S(1)} fusion(f32[1984,2048]{1,0:T(8,128)} %param.7, f32[1984,256]{1,0:T(8,128)S(1)} %copy-done), kind=kOutput, calls=%fused_computation.60 | convolution fusion | flops 6241124352 | bytes 20381696 | tf_op jit(solution)/shard_map/jc,jr->cr/dot_general | solution.py:319
  28.2 162.3 %shard_map.74 = (f32[32,88,256]{2,1,0:T(8,128)S(1)}, f32[2,2,2,4,2,32,256]{6,5,4,3,2,1,0:T(8,128)S(1)}, s32[2,2,4,2,8,128]{5,4,3,2,1,0:T(8,128)S(1)}) custom-call(f32[2,2,2,4,2,32,256]{6,5,4,3,2,1,0:T(8,128)S(1)} %bitcast.32, f32[32,1024]{1,0:T(8,128)S(1)} %copy-done.4, f32[2,32,1024]{2,1,0:T(8,128)S(1)} %copy-done.3, f32[2,32,256]{2,1,0:T(8,128)S(1)} %copy-done.5, ...), custom_call_target="tpu_custom_call" | custom-call | tf_op jit(solution)/shard_map/pallas_call | solution.py:192
  190.5 0.0 copy-start.1
  190.6 1.3 copy-done.1
  191.9 0.1 sub.43
  192.0 0.1 add_reduce_fusion
  192.1 0.1 sub.39
  192.1 0.1 compare_reduce_fusion
  192.2 0.1 gt.12
  192.3 0.1 and.35
  192.5 1.6 copy-done.2
  194.1 19.8 %shard_map.75 = f32[2048,256]{1,0:T(8,128)} custom-call(s32[2816]{0:T(1024)S(1)} %and_select_fusion.tail_slots, s32[2048]{0:T(1024)S(1)} %and_select_fusion.1.head_slots, f32[2816,256]{1,0:T(8,128)S(1)} %bitcast.34, f32[2048,256]{1,0:T(8,128)S(1)} %bitcast.35), custom_call_target="tpu_custom_call" | custom-call | tf_op jit(solution)/shard_map/pallas_call | solution.py:269
  (18 shorter events, 0.2 us)
Async XLA Ops:
  0.8 2.8 %copy-start = (f32[1984,256]{1,0:T(8,128)S(1)}, f32[1984,256]{1,0:T(8,128)}, u32[]{:S(2)}) copy-start(f32[1984,256]{1,0:T(8,128)} %rows.1) | copy-start | bytes 6094852
  11.3 16.9 %copy-start.6 = (s32[2,32]{1,0:T(2,128)S(1)}, s32[2,32]{1,0:T(2,128)}, u32[]{:S(2)}) copy-start(s32[2,32]{1,0:T(2,128)} %param.12) | copy-start | bytes 772
  11.3 16.9 %copy-start.3 = (f32[2,32,1024]{2,1,0:T(8,128)S(1)}, f32[2,32,1024]{2,1,0:T(8,128)}, u32[]{:S(2)}) copy-start(f32[2,32,1024]{2,1,0:T(8,128)} %diag.1) | copy-start | bytes 786436
  11.3 16.9 %copy-start.4 = (f32[32,1024]{1,0:T(8,128)S(1)}, f32[32,1024]{1,0:T(8,128)}, u32[]{:S(2)}) copy-start(f32[32,1024]{1,0:T(8,128)} %link.1) | copy-start | bytes 393220
  11.3 16.9 %copy-start.5 = (f32[2,32,256]{2,1,0:T(8,128)S(1)}, f32[2,32,256]{2,1,0:T(8,128)}, u32[]{:S(2)}) copy-start(f32[2,32,256]{2,1,0:T(8,128)} %rhs.5) | copy-start | bytes 196612
  190.5 1.3 copy-start.1
  192.5 1.6 copy-start.2

commit v2 on v1

--- a/solution.py
+++ b/solution.py
@@ -1,4 +1,6 @@
 import functools
+import itertools
+import math
 
 import jax
 import jax.numpy as jnp
@@ -8,6 +10,9 @@
 from jax.sharding import PartitionSpec as P
 
 AXES = ("prow", "pcol")
+DIMS = "xczy"
+LEVELS = ("c", "xy", "z")
+BULK = 3
 MESH = pl.DeviceIdType.MESH
 HIGHEST = lax.Precision.HIGHEST
 
@@ -38,80 +43,74 @@
     x, core = prow // cores, prow % cores
     z, y = pcol // ys, pcol % ys
 
-    def at_core(v):
-        return (x * cores + v, pcol)
-
-    def at_x(v):
-        return (v * cores + core, pcol)
-
-    def at_y(v):
-        return (prow, z * ys + v)
-
-    def at_z(v):
-        return (prow, v * ys + y)
-
-    coords = {"c": (core, cores, at_core), "x": (x, xs, at_x), "y": (y, ys, at_y), "z": (z, zs, at_z)}
+    coord = {"x": x, "c": core, "z": z, "y": y}
+    extent = {"x": xs, "c": cores, "z": zs, "y": ys}
     counter = [0]
-
-    def remote(src, dst, device):
+    sent = [1]
+
+    def more(count):
+        first, last = sent[0], min(sent[0] + count, devices)
+        sent[0] = last
+        if last > first:
+            lax.fori_loop(first, last, move_start, 0)
+
+    def remote(src, dst, place):
         k = counter[0]
         counter[0] += 1
         copy = pltpu.make_async_remote_copy(
             src_ref=src, dst_ref=dst, send_sem=send_sems.at[k], recv_sem=recv_sems.at[k],
-            device_id=device, device_id_type=MESH,
+            device_id=(place["x"] * cores + place["c"], place["z"] * ys + place["y"]),
+            device_id_type=MESH,
         )
         copy.start()
         return copy
 
-    def reduce_start(axis, source, cut, landing):
-        me, size, place = coords[axis]
-        return [
-            remote(cut(source, (me + d) % size), landing.at[d - 1], place((me + d) % size))
-            for d in range(1, size)
-        ]
-
-    def gather_start(axis, ref):
-        size = coords[axis][1]
-        me, _, place = coords[axis]
-        part = {
-            "z": ref.at[x, core, z, y],
-            "y": ref.at[x, core, :, y],
-            "x": ref.at[x, core],
-            "c": ref.at[:, core],
-        }[axis]
-        return [remote(part, part, place((me + d) % size)) for d in range(1, size)]
+    def peers(group):
+        found = []
+        for offsets in itertools.product(*[range(extent[a]) for a in group]):
+            if any(offsets):
+                place = dict(coord)
+                for a, d in zip(group, offsets):
+                    place[a] = (coord[a] + d) % extent[a]
+                found.append(place)
+        return found
+
+    def cut(dims, group, place):
+        return tuple(place[a] if a in group else slice(None) for a in dims)
+
+    def gather_start(step, ref):
+        group = LEVELS[::-1][step]
+        waiting = "".join(LEVELS[: len(LEVELS) - step])
+        part = ref.at[cut(DIMS, waiting, coord)]
+        return [remote(part, part, place) for place in peers(group)]
 
     def finish(copies):
         for copy in copies:
             copy.wait()
 
-    cuts = {
-        "c": lambda ref, v: ref.at[:, v],
-        "x": lambda ref, v: ref.at[v],
-        "y": lambda ref, v: ref.at[:, v],
-        "z": lambda ref, v: ref.at[v],
-    }
-    reads = {
-        "c": lambda ref: ref[:, core],
-        "x": lambda ref: ref[x],
-        "y": lambda ref: ref[:, y],
-        "z": lambda ref: ref[z],
-    }
+    def gather(ref):
+        for step in range(len(LEVELS)):
+            copies = gather_start(step, ref)
+            more(BULK)
+            finish(copies)
 
     def reduce_levels(source, landings, sums, beside):
-        current = source
-        for step, axis in enumerate("cxyz"):
-            size = coords[axis][1]
-            copies = reduce_start(axis, current, cuts[axis], landings[step])
-            others = [gather_start("zyxc"[step], ref) for ref in beside]
+        current, dims = source, DIMS
+        for step, group in enumerate(LEVELS):
+            copies = [
+                remote(current.at[cut(dims, group, place)], landings[step].at[n], place)
+                for n, place in enumerate(peers(group))
+            ]
+            others = [gather_start(step, ref) for ref in beside]
+            more(BULK)
             finish(copies)
-            total = reads[axis](current)
-            for d in range(1, size):
-                total = total + landings[step][d - 1]
+            total = current[cut(dims, group, coord)]
+            for n in range(len(copies)):
+                total = total + landings[step][n]
             sums[step][...] = total
-            for more in others:
-                finish(more)
-            current = sums[step]
+            for some in others:
+                finish(some)
+            current, dims = sums[step], "".join(a for a in dims if a not in group)
         return current
 
     barrier = pltpu.get_barrier_semaphore()
@@ -144,13 +143,11 @@
 
     own = pltpu.make_async_copy(outgoing.at[position], received.at[position], own_sem)
     own.start()
-    lax.fori_loop(1, devices, move_start, 0)
 
     all_pivots[x, core, z, y] = pivots[...]
     reduced = reduce_levels(terms.at[1], up_recv, up_sum, [all_pivots])
     full_upper[x, core, z, y] = rhs[1] - reduced[...]
-    for axis in "zyxc":
-        finish(gather_start(axis, full_upper))
+    gather(full_upper)
     rows = devices * rhs.shape[1]
     columns = rhs.shape[2]
     upper = dot32(diag[1], full_upper[...].reshape(rows, columns), ((1,), (0,)))
@@ -158,12 +155,11 @@
     base[...] = terms[0] + dot32(link[...], upper, ((0,), (0,))).reshape(base.shape)
     reduced = reduce_levels(base, low_recv, low_sum, [heads.at[1]])
     full_lower[x, core, z, y] = rhs[0] - reduced[...]
-    for axis in "zyxc":
-        finish(gather_start(axis, full_lower))
+    gather(full_lower)
     heads[0, x, core, z, y] = dot32(diag[0], full_lower[...].reshape(rows, columns), ((1,), (0,)))
-    for axis in "zyxc":
-        finish(gather_start(axis, heads.at[0]))
-
+    gather(heads.at[0])
+
+    more(devices)
     own.wait()
     lax.fori_loop(1, devices, move_wait, 0)
 
@@ -173,20 +169,23 @@
     devices = xs * cores * zs * ys
     _, share, columns = rhs.shape
     tail = (share, columns)
-    landings = lambda: [
-        pltpu.VMEM((max(cores - 1, 1), xs, zs, ys) + tail, jnp.float32),
-        pltpu.VMEM((max(xs - 1, 1), zs, ys) + tail, jnp.float32),
-        pltpu.VMEM((max(ys - 1, 1), zs) + tail, jnp.float32),
-        pltpu.VMEM((max(zs - 1, 1),) + tail, jnp.float32),
-    ]
-    sums = lambda: [
-        pltpu.VMEM((xs, zs, ys) + tail, jnp.float32),
-        pltpu.VMEM((zs, ys) + tail, jnp.float32),
-        pltpu.VMEM((zs,) + tail, jnp.float32),
-        pltpu.VMEM(tail, jnp.float32),
-    ]
+    extent = {"x": xs, "c": cores, "z": zs, "y": ys}
+
+    def buffers():
+        landings, sums, dims, peers = [], [], DIMS, 0
+        for group in LEVELS:
+            dims = "".join(a for a in dims if a not in group)
+            others = math.prod(extent[a] for a in group) - 1
+            shape = tuple(extent[a] for a in dims) + tail
+            landings.append(pltpu.VMEM((max(others, 1),) + shape, jnp.float32))
+            sums.append(pltpu.VMEM(shape, jnp.float32))
+            peers += others
+        return landings, sums, peers
+
+    up_recv, up_sum, peers = buffers()
+    low_recv, low_sum, _ = buffers()
     whole = (xs, cores, zs, ys) + tail
-    copies = 7 * ((cores - 1) + (xs - 1) + (zs - 1) + (ys - 1))
+    copies = 7 * peers
     vmem = pl.BlockSpec(memory_space=pltpu.VMEM)
     anywhere = pl.BlockSpec(memory_space=pl.ANY)
     return pl.pallas_call(
@@ -203,7 +202,7 @@
             pltpu.VMEM(whole, jnp.float32),
             pltpu.VMEM(whole, jnp.float32),
             pltpu.VMEM(tail, jnp.float32),
-            landings(), sums(), landings(), sums(),
+            up_recv, up_sum, low_recv, low_sum,
             pltpu.SemaphoreType.DMA((copies,)),
             pltpu.SemaphoreType.DMA((copies,)),
             pltpu.SemaphoreType.DMA((devices,)),
@@ -245,18 +244,21 @@
     )(slots, rows, index_rows)
 
 
-def unpack_kernel(tail_slots, head_slots, received, heads, out, held, sem):
-    def place(slots, source):
+def unpack_kernel(tail_slots, head_slots, tail_used, head_used, received, heads, out, held, sem):
+    def place(slots, used, source):
         def step(group, carry):
-            start = pl.multiple_of(group * 8, 8)
-            for k in range(8):
-                held[pl.ds(slots[start + k], 1), :] = source[pl.ds(start + k, 1), :]
+            @pl.when(used[group] > 0)
+            def _():
+                start = pl.multiple_of(group * 8, 8)
+                for k in range(8):
+                    held[pl.ds(slots[start + k], 1), :] = source[pl.ds(start + k, 1), :]
+
             return carry
 
         lax.fori_loop(0, source.shape[0] // 8, step, 0)
 
-    place(tail_slots, received)
-    place(head_slots, heads)
+    place(tail_slots, tail_used, received)
+    place(head_slots, head_used, heads)
     copy = pltpu.make_async_copy(held.at[pl.ds(0, out.shape[0])], out, sem)
     copy.start()
     copy.wait()
@@ -266,14 +268,18 @@
     columns = heads.shape[1]
     smem = pl.BlockSpec(memory_space=pltpu.SMEM)
     vmem = pl.BlockSpec(memory_space=pltpu.VMEM)
+
+    def used(slots):
+        return jnp.any(slots.reshape(-1, 8) < rows_each, axis=1).astype(jnp.int32)
+
     return pl.pallas_call(
         unpack_kernel,
         out_shape=jax.ShapeDtypeStruct((rows_each, columns), jnp.float32),
-        in_specs=[smem, smem, vmem, vmem],
+        in_specs=[smem] * 4 + [vmem, vmem],
         out_specs=pl.BlockSpec(memory_space=pl.ANY),
         scratch_shapes=[pltpu.VMEM((rows_each + 8, columns), jnp.float32), pltpu.SemaphoreType.DMA],
         compiler_params=pltpu.CompilerParams(vmem_limit_bytes=24 * 2**20),
-    )(tail_slots, head_slots, received, heads)
+    )(tail_slots, head_slots, used(tail_slots), used(head_slots), received, heads)
 
 
 def ranks_of(one_hot):

time: 214 us -> 174 us (0.81)
  Pallas kernels: 190 us -> 149 us
    pallas_call x1, Pallas kernels: 162 us -> 123 us  [sweep_call(): pl.pallas_call(functools.partial(sweep_kernel, sizes), out_shape=(jax.Sha...]
where the time goes in v2:
time: 174 us; the launch traced here: 173 us
  Pallas kernels  149 us (86%)
  matrix products  18.5 us (11%)
  local copies, waits for them, and re-layouts  3.78 us (2%)
  other arithmetic  2.21 us (1%)
    pallas_call x1, Pallas kernels, sweep_call(): pl.pallas_call(functools.partial(sweep_kernel, sizes), out_shape=(jax.Sha...  123 us
    pallas_call x1, Pallas kernels, unpack_call(): pl.pallas_call(unpack_kernel, out_shape=jax.ShapeDtypeStruct((rows_each,...  18.2 us
    dot_general x1, matrix products, body(): jnp.einsum('jc,jr->cr', tail_factor, tail_solution, precision=lax.Precisi...  16.8 us
    pallas_call x1, Pallas kernels, pack_call(): pl.pallas_call(functools.partial(pack_kernel, capacity), out_shape=jax.Sh...  7.73 us

profile of v2, /device:TPU:0, one launch (start us, length us, event | category | flops | bytes accessed | tf_op | source)
XLA Modules:
  0.0 173.5 jit_solution(7696738152615110)
XLA Ops:
  0.0 0.7 add_select_fusion.3
  0.8 0.1 convert_reduce_fusion
  1.0 0.3 fusion.2
  1.2 0.8 add_select_fusion
  2.1 0.7 convolution_multiply_fusion
  2.8 0.7 convolution_add_fusion.1.index_rows
  3.5 7.7 %shard_map.73 = f32[2816,256]{1,0:T(8,128)S(1)} custom-call(s32[1984]{0:T(1024)S(1)} %get-tuple-element.16.slots, f32[1984,256]{1,0:T(8,128)S(1)} %copy-done, f32[32,256]{1,0:T(8,128)S(1)} %convolution_add_fusion.1.index_rows), custom_call_target="tpu_custom_call" | custom-call | tf_op jit(solution)/shard_map/pallas_call | solution.py:234
  11.3 16.8 %fusion.34 = f32[2048,256]{1,0:T(8,128)S(1)} fusion(f32[1984,2048]{1,0:T(8,128)} %param.7, f32[1984,256]{1,0:T(8,128)S(1)} %copy-done), kind=kOutput, calls=%fused_computation.69 | convolution fusion | flops 6241124352 | bytes 20381696 | tf_op jit(solution)/shard_map/jc,jr->cr/dot_general | solution.py:325
  28.2 122.8 %shard_map.74 = (f32[32,88,256]{2,1,0:T(8,128)S(1)}, f32[2,2,2,4,2,32,256]{6,5,4,3,2,1,0:T(8,128)S(1)}, s32[2,2,4,2,8,128]{5,4,3,2,1,0:T(8,128)S(1)}) custom-call(f32[2,2,2,4,2,32,256]{6,5,4,3,2,1,0:T(8,128)S(1)} %bitcast.42, f32[32,1024]{1,0:T(8,128)S(1)} %copy-done.4, f32[2,32,1024]{2,1,0:T(8,128)S(1)} %copy-done.3, f32[2,32,256]{2,1,0:T(8,128)S(1)} %copy-done.5, ...), custom_call_target="tpu_custom_call" | custom-call | tf_op jit(solution)/shard_map/pallas_call | solution.py:191
  151.0 1.3 copy-done.1
  152.4 0.1 copy.17
  152.5 0.1 fusion.33
  152.6 0.1 copy.16
  152.7 0.1 fusion.16
  152.8 0.1 copy.18
  152.9 0.1 reshape.82.tail_used
  153.1 0.1 sub.52
  153.1 0.1 fusion.13
  153.3 0.1 sub.46
  153.4 0.1 gt.20
  153.5 0.1 and.47
  153.6 0.1 sub.50
  153.7 1.6 copy-done.2
  155.3 18.2 %shard_map.75 = f32[2048,256]{1,0:T(8,128)} custom-call(s32[2816]{0:T(1024)S(1)} %and_select_fusion.tail_slots, s32[2048]{0:T(1024)S(1)} %and_select_fusion.1.head_slots, s32[352]{0:T(512)S(1)} %reshape.82.tail_used, s32[256]{0:T(256)S(1)} %convert_element_type.42.head_used, f32[2816,256]{1,0:T(8,128)S(1)} %bitcast.44, f32[2048,256]{1,0:T(8,128)S(1)} %bitcast.45), custom_call_target="tpu_custom_call" | custom-call | tf_op jit(solution)/shard_map/pallas_call | solution.py:275
  (28 shorter events, 0.3 us)
Async XLA Ops:
  0.8 2.8 %copy-start = (f32[1984,256]{1,0:T(8,128)S(1)}, f32[1984,256]{1,0:T(8,128)}, u32[]{:S(2)}) copy-start(f32[1984,256]{1,0:T(8,128)} %rows.1) | copy-start | bytes 6094852
  11.3 16.9 %copy-start.6 = (s32[2,32]{1,0:T(2,128)S(1)}, s32[2,32]{1,0:T(2,128)}, u32[]{:S(2)}) copy-start(s32[2,32]{1,0:T(2,128)} %param.12) | copy-start | bytes 772
  11.3 16.9 %copy-start.3 = (f32[2,32,1024]{2,1,0:T(8,128)S(1)}, f32[2,32,1024]{2,1,0:T(8,128)}, u32[]{:S(2)}) copy-start(f32[2,32,1024]{2,1,0:T(8,128)} %diag.1) | copy-start | bytes 786436
  11.3 16.9 %copy-start.4 = (f32[32,1024]{1,0:T(8,128)S(1)}, f32[32,1024]{1,0:T(8,128)}, u32[]{:S(2)}) copy-start(f32[32,1024]{1,0:T(8,128)} %link.1) | copy-start | bytes 393220
  11.3 16.9 %copy-start.5 = (f32[2,32,256]{2,1,0:T(8,128)S(1)}, f32[2,32,256]{2,1,0:T(8,128)}, u32[]{:S(2)}) copy-start(f32[2,32,256]{2,1,0:T(8,128)} %rhs.5) | copy-start | bytes 196612
  151.0 1.3 copy-start.1
  153.7 1.6 copy-start.2
